TPU v7x, 32 devices: a whole 2x2x4 slice. The times are simulated.
32 devices in a mesh: groups: 2 (over y), row: 8 (over z, core), col: 2 (over x).
Axes of the slice: x: 2, y: 2, z: 4, core: 2. Of those that a mesh axis runs over, the one named last changes fastest.
Arguments:
- homolog_features: bfloat16 [32, 256, 256], P(('groups', 'row'), 'col'), parts along dimension 0, may hold values from -6 to 6
- couple_features: bfloat16 [512, 256, 128], P(('groups', 'col'), 'row'), parts along dimension 0, may hold values from -6 to 6
- strand_start_amino: int32 [8], P('groups'), parts along dimension 0, may hold values from 0 to 192, as said below
- homolog_strand_label: int32 [32], P('groups'), parts along dimension 0, may hold values from 0 to 4, as said below
- tensor_product_source: bfloat16 [256, 32], replicated, may hold values from -0.375 to 0.375
- tensor_product_target: bfloat16 [256, 32], replicated, may hold values from -0.375 to 0.375
- tensor_product_final: bfloat16 [1024, 128], replicated, may hold values from -1 to 1
- couple_offset_tensor: float32 [128, 8], replicated
- probe_tensor: bfloat16 [256, 256], replicated, may hold values from -0.375 to 0.375
- lookup_content_tensor: bfloat16 [256, 512], replicated, may hold values from -0.375 to 0.375
- sigmoid_factor_tensor: bfloat16 [256, 256], replicated, may hold values from -0.375 to 0.375
- heads_merge_tensor: bfloat16 [256, 256], replicated, may hold values from -0.75 to 0.75
Outputs:
- refreshed_homologs: bfloat16 [32, 256, 256], P(('groups', 'row'), 'col'), parts along dimension 0
- pair_output_state: bfloat16 [512, 256, 128], P(('groups', 'col'), 'row'), parts along dimension 0
There are 2 independent parts, one for each index of `groups`. A program takes and returns all parts, laid end to end along the dimension named above; an argument that names none is the same for every part. Nothing has to cross between parts.
Inputs may be any that keep to these rules, and one draw needn't show every extreme that they name: `strand_start_amino`: strictly increasing with first entry 0 and last entry 192; chain k holds residues from entry k up to the next entry, the last chain up to 255. `homolog_strand_label`: a row with value 4 is paired and covers all residues; a row with value k covers chain k only; at least 8 rows are paired and every chain has a row of its own.
All inputs are finite; a program needn't handle non-finite values.
Results may differ from a plain program's by a relative error of at most 0.025.
The roundings to bfloat16 on the way count: a program that leaves them out, or rounds other values in their place, can miss the bound.
Values may be sent and summed in bfloat16 or wider, within the bound.
A program may use at most 128 MiB of HBM per device.

v0:
```python
import math

import jax
import jax.numpy as jnp
from jax import lax
from jax.sharding import PartitionSpec as P

EPS = 1e-05


def standardize_features(values):
    values = values.astype(jnp.float32)
    center = values - jnp.mean(values, axis=-1, keepdims=True)
    spread = jnp.mean(center * center, axis=-1, keepdims=True)
    return center * lax.rsqrt(spread + EPS)


def linear_transform(values, weight):
    flattened = values.reshape(-1, values.shape[-1])
    result = jnp.dot(flattened, weight, preferred_element_type=jnp.float32)
    return result.reshape(values.shape[:-1] + (weight.shape[1],))


def alignment_row_mask(row_chain, position, strand_start_amino):
    chains = strand_start_amino.shape[0]
    owning = (
        jnp.sum((position[:, None] >= strand_start_amino[None, :]).astype(jnp.int32), axis=1) - 1
    )
    kept_entry = (row_chain[:, None] == chains) | (row_chain[:, None] == owning[None, :])
    return kept_entry.astype(jnp.float32)


def outer_update(left_block, right_rows, count_block, pair_block, tensor_product_final):
    collected_homologs, rows_here, width = left_block.shape
    cols_here = right_rows.shape[1]
    left_matrix = left_block.transpose(1, 2, 0).reshape(rows_here * width, collected_homologs)
    right_matrix = right_rows.reshape(collected_homologs, cols_here * width)
    outer = jnp.dot(left_matrix, right_matrix, preferred_element_type=jnp.float32).astype(
        jnp.bfloat16
    )
    outer = outer.reshape(rows_here, width, cols_here, width).transpose(0, 2, 1, 3)
    outer = outer.reshape(rows_here * cols_here, width * width)
    update = jnp.dot(outer, tensor_product_final, preferred_element_type=jnp.float32).reshape(
        rows_here, cols_here, -1
    )
    return (pair_block.astype(jnp.float32) + update / (count_block[:, :, None] + 0.001)).astype(
        jnp.bfloat16
    )


def per_device(
    homolog_features,
    couple_features,
    strand_start_amino,
    homolog_strand_label,
    tensor_product_source,
    tensor_product_target,
    tensor_product_final,
    couple_offset_tensor,
    probe_tensor,
    lookup_content_tensor,
    sigmoid_factor_tensor,
    heads_merge_tensor,
):
    homolog_enumeration, held_amino_range = (homolog_features.shape[0], homolog_features.shape[1])
    cols_pair = couple_features.shape[1]
    collected_homologs = homolog_strand_label.shape[0]
    heads = couple_offset_tensor.shape[1]
    inner = probe_tensor.shape[1]
    head_dim = inner // heads
    row_location = lax.axis_index("row")
    col_place = lax.axis_index("col")
    chain_of_local_rows = lax.dynamic_slice_in_dim(
        homolog_strand_label, row_location * homolog_enumeration, homolog_enumeration, 0
    )
    owned_residue_positions = col_place * held_amino_range + jnp.arange(
        held_amino_range, dtype=jnp.int32
    )
    paired_residue_positions = row_location * cols_pair + jnp.arange(cols_pair, dtype=jnp.int32)
    mask_for_local = alignment_row_mask(
        chain_of_local_rows, owned_residue_positions, strand_start_amino
    )
    standardized_homologs = standardize_features(homolog_features).astype(jnp.bfloat16)
    local_left_rows = (
        linear_transform(standardized_homologs, tensor_product_source) * mask_for_local[:, :, None]
    ).astype(jnp.bfloat16)
    local_right_rows = (
        linear_transform(standardized_homologs, tensor_product_target) * mask_for_local[:, :, None]
    ).astype(jnp.bfloat16)
    gathered_left_rows, right_band = (
        lax.all_gather(local_left_rows, "row", axis=0, tiled=True),
        lax.all_gather(local_right_rows, "row", axis=0, tiled=True),
    )
    right_wide = lax.all_gather(right_band, "col", axis=1, tiled=True)
    right_rows = lax.dynamic_slice_in_dim(right_wide, row_location * cols_pair, cols_pair, 1)
    row_side_mask = alignment_row_mask(
        homolog_strand_label, owned_residue_positions, strand_start_amino
    )
    column_side_mask = alignment_row_mask(
        homolog_strand_label, paired_residue_positions, strand_start_amino
    )
    count = jnp.dot(
        row_side_mask.T,
        column_side_mask,
        precision=lax.Precision.HIGHEST,
        preferred_element_type=jnp.float32,
    )
    block = min(held_amino_range, 128)
    blocks = held_amino_range // block
    left_blocks = gathered_left_rows.reshape(collected_homologs, blocks, block, -1).transpose(
        1, 0, 2, 3
    )
    count_blocks = count.reshape(blocks, block, cols_pair)
    pair_blocks = couple_features.reshape(blocks, block, cols_pair, -1)

    def one_block(inputs):
        left_block, count_block, pair_block = inputs
        pair_new = outer_update(
            left_block, right_rows, count_block, pair_block, tensor_product_final
        )
        pair_normed = standardize_features(pair_new).astype(jnp.bfloat16)
        bias_new = jnp.dot(
            pair_normed.reshape(-1, pair_normed.shape[-1]).astype(jnp.float32),
            couple_offset_tensor,
            precision=lax.Precision.HIGHEST,
            preferred_element_type=jnp.float32,
        )
        return (pair_new, bias_new.astype(jnp.bfloat16).reshape(block, cols_pair, heads))

    pair_parts, bias_parts = lax.map(one_block, (left_blocks, count_blocks, pair_blocks))
    pair_output_state = pair_parts.reshape(held_amino_range, cols_pair, -1)
    bias_local = bias_parts.reshape(held_amino_range, cols_pair, heads).transpose(2, 0, 1)
    bias_full = lax.all_gather(bias_local, "row", axis=2, tiled=True)
    query_vectors = (
        linear_transform(standardized_homologs, probe_tensor)
        .astype(jnp.bfloat16)
        .reshape(homolog_enumeration, held_amino_range, heads, head_dim)
    )
    gate_signal = jax.nn.sigmoid(linear_transform(standardized_homologs, sigmoid_factor_tensor))
    scale = 1.0 / math.sqrt(head_dim)
    local_key_value = linear_transform(standardized_homologs, lookup_content_tensor).astype(
        jnp.bfloat16
    )
    keyval_piece = lax.all_gather(local_key_value, "col", axis=1, tiled=True)
    running_max = jnp.full((homolog_enumeration, heads, held_amino_range), -1e30, jnp.float32)
    count_here = keyval_piece.shape[1]
    keys = keyval_piece[:, :, :inner].reshape(homolog_enumeration, count_here, heads, head_dim)
    vals = keyval_piece[:, :, inner:].reshape(homolog_enumeration, count_here, heads, head_dim)
    scores = (
        jnp.einsum("sihd,sjhd->shij", query_vectors, keys, preferred_element_type=jnp.float32)
        * scale
    )
    residue_positions = jnp.arange(count_here, dtype=jnp.int32)
    key_mask = alignment_row_mask(chain_of_local_rows, residue_positions, strand_start_amino)
    scores = (
        scores
        + bias_full.astype(jnp.float32)[None]
        + ((key_mask - 1.0) * 1000000000.0)[:, None, None, :]
    )
    new_max = jnp.maximum(running_max, jnp.max(scores, axis=-1))
    weights = jnp.exp(scores - new_max[..., None])
    running_sum = jnp.sum(weights, axis=-1)
    weighted = jnp.einsum(
        "shij,sjhd->shid", weights.astype(jnp.bfloat16), vals, preferred_element_type=jnp.float32
    )
    running_max, running_sum, weighted = (new_max, running_sum, weighted)
    attended = (
        (weighted / running_sum[..., None])
        .transpose(0, 2, 1, 3)
        .reshape(homolog_enumeration, held_amino_range, inner)
    )
    sigmoid_scaled_result = (gate_signal * attended).astype(jnp.bfloat16)
    refreshed_homologs = (
        homolog_features.astype(jnp.float32)
        + linear_transform(sigmoid_scaled_result, heads_merge_tensor)
    ).astype(jnp.bfloat16)
    return (refreshed_homologs, pair_output_state)


def solution(mesh):
    placed = (
        P(("groups", "row"), "col", None),
        P(("groups", "col"), "row", None),
        P("groups"),
        P("groups"),
        P(),
        P(),
        P(),
        P(),
        P(),
        P(),
        P(),
        P(),
    )
    return jax.shard_map(
        per_device,
        mesh=mesh,
        in_specs=placed,
        out_specs=(P(("groups", "row"), "col", None), P(("groups", "col"), "row", None)),
        check_vma=False,
    )
```

profile of v0, /device:TPU:1, one launch (start us, length us, event | category | flops | bytes accessed | tf_op | source)
XLA Modules:
  0.0 179.0 jit_solution(15756423830798715271)
XLA Ops:
  0.6 0.0 copy-start
  0.7 0.8 broadcast_compare_fusion.1
  1.4 0.7 convert_reduce_fusion.4
  2.2 0.1 or_convert_fusion.1
  2.3 1.0 convert_reduce_fusion.1
  3.3 1.1 fusion.19
  4.4 1.2 fusion.14
  5.6 15.6 %all_gather.17 = bf16[16,128,32]{1,2,0:T(8,128)(2,1)S(1)} all-gather(bf16[2,128,32]{1,2,0:T(8,128)(2,1)S(1)} %fusion.14), channel_id=1, replica_groups=mesh['groups'=2,'row'=8,'col'=2] {'row'}, dimensions={0}, use_global_device_ids=true | all-gather | bytes 147456 | tf_op jit(solution)/shard_map/all_gather | solution.py:92
  21.1 5.6 %all_gather.18 = bf16[16,256,32]{1,2,0:T(8,128)(2,1)S(1)} all-gather(bf16[16,128,32]{1,2,0:T(8,128)(2,1)S(1)} %all_gather.17), channel_id=1, replica_groups=mesh['groups'=2,'row'=8,'col'=2] {'col'}, dimensions={1}, use_global_device_ids=true | all-gather | bytes 393216 | tf_op jit(solution)/shard_map/all_gather | solution.py:94
  26.7 0.1 constant_dynamic-slice_fusion
  26.8 0.1 copy.62
  26.9 0.2 reshape.215
  27.1 1.2 fusion.13
  28.3 14.9 %all_gather.16 = bf16[16,128,32]{1,2,0:T(8,128)(2,1)S(1)} all-gather(bf16[2,128,32]{1,2,0:T(8,128)(2,1)S(1)} %fusion.13), channel_id=1, replica_groups=mesh['groups'=2,'row'=8,'col'=2] {'row'}, dimensions={0}, use_global_device_ids=true | all-gather | bytes 147456 | tf_op jit(solution)/shard_map/all_gather | solution.py:91
  43.2 0.3 copy.61
  43.5 0.5 reshape.214
  44.0 5.6 %convolution_convert_fusion = bf16[4096,1024]{1,0:T(8,128)(2,1)} fusion(bf16[4096,16]{0,1:T(8,128)(2,1)S(1)} %reshape.214, bf16[16,1024]{1,0:T(8,128)(2,1)S(1)} %reshape.215), kind=kOutput, calls=%fused_computation | convolution fusion | flops 138412032 | bytes 8552448 | tf_op jit(solution)/shard_map/while/body/eval_jaxpr/dot_general | solution.py:38
  49.6 39.1 %reshape.216 = bf16[128,32,32,32]{3,2,1,0:T(8,128)(2,1)} reshape(bf16[4096,1024]{1,0:T(8,128)(2,1)} %convolution_convert_fusion) | data formatting | bytes 16777216 | tf_op jit(solution)/shard_map/while/body/eval_jaxpr/reshape | solution.py:41
  88.7 39.3 %copy.63 = bf16[128,32,32,32]{0,3,2,1:T(8,128)(2,1)} copy(bf16[128,32,32,32]{3,1,2,0:T(8,128)(2,1)} %bitcast.50) | data formatting | bytes 16777216 | tf_op jit(solution)/shard_map/while/body/eval_jaxpr/transpose | solution.py:41
  128.0 0.1 convert_reduce_fusion.3
  128.1 0.3 convolution_add_fusion.1
  128.4 6.9 %convert_reduce_fusion = (f32[128,32]{0,1:T(8,128)S(1)}, bf16[128,32,128]{2,0,1:T(8,128)(2,1)S(1)}) fusion(f32[128,32]{0,1:T(8,128)S(1)} %convolution_add_fusion.1, bf16[128,32,1024]{0,2,1:T(8,128)(2,1)} %bitcast.51, bf16[1024,128]{1,0:T(8,128)(2,1)S(1)} %copy-done, bf16[128,32,128]{2,1,0:T(8,128)(2,1)S(1)} %copy-done.7), kind=kOutput, calls=%fused_computation.3 | convolution fusion | flops 1076883456 | bytes 10780672 | tf_op jit(solution)/shard_map/while/body/eval_jaxpr/dot_general | solution.py:43
  135.3 1.3 fusion.2
  136.6 0.0 copy-start.4
  136.6 1.2 fusion.3
  137.9 0.7 copy.65
  138.5 0.0 copy-start.1
  138.6 0.0 copy-start.2
  138.6 0.9 convolution_convert_fusion.1
  139.5 0.2 reshape.218
  139.7 0.1 copy.66
  139.8 14.9 %all_gather.19 = bf16[8,128,256]{1,0,2:T(8,128)(2,1)S(1)} all-gather(bf16[8,128,32]{1,0,2:T(8,128)(2,1)S(1)} %copy.66), channel_id=1, replica_groups=mesh['groups'=2,'row'=8,'col'=2] {'row'}, dimensions={2}, use_global_device_ids=true | all-gather | bytes 589824 | tf_op jit(solution)/shard_map/all_gather | solution.py:133
  154.8 1.3 copy.67
  156.1 0.1 convert_reduce_fusion.2
  156.2 0.1 fusion.47
  156.3 0.3 convolution_convert_fusion.2
  156.5 8.4 %all_gather.15 = bf16[2,256,512]{2,1,0:T(8,128)(2,1)S(1)} all-gather(bf16[2,128,512]{2,1,0:T(8,128)(2,1)S(1)} %convolution_convert_fusion.2), channel_id=1, replica_groups=mesh['groups'=2,'row'=8,'col'=2] {'col'}, dimensions={1}, use_global_device_ids=true | all-gather | bytes 786432 | tf_op jit(solution)/shard_map/all_gather | solution.py:144
  165.0 0.7 fusion.49
  165.7 0.8 copy.59
  166.6 0.3 convolution_convert_fusion.3
  166.8 0.8 copy.58
  167.6 2.0 %fusion.50 = (f32[2,8,128]{2,1,0:T(8,128)S(1)}, f32[2,8,128,256]{3,2,1,0:T(8,128)S(1)}) fusion(f32[2,256]{1,0:T(2,128)S(1)} %fusion.47, f32[8,128,256]{2,1,0:T(8,128)} %copy.67, bf16[2,128,8,32]{1,3,2,0:T(8,128)(2,1)} %bitcast.57, bf16[2,256,8,32]{1,3,2,0:T(8,128)(2,1)} %bitcast.53), kind=kOutput, calls=%fused_computation.78 | convolution fusion | flops 35649536 | bytes 3549184 | tf_op jit(solution)/shard_map/sihd,sjhd->shij/dot_general | solution.py:150
  169.6 0.6 fusion.4
  170.2 1.8 %copy.68 = bf16[2,256,256]{1,2,0:T(8,128)(2,1)} copy(bf16[2,256,256]{2,1,0:T(8,128)(2,1)} %get-tuple-element.42) | data formatting | bytes 524288 | tf_op jit(solution)/shard_map/slice | solution.py:148
  172.0 2.2 %fusion.10 = f32[2,128,8,32]{1,3,2,0:T(8,128)} fusion(bf16[2,256,8,32]{1,3,2,0:T(8,128)(2,1)} %bitcast.54, f32[2,8,128,256]{3,2,1,0:T(8,128)S(1)} %get-tuple-element.46, f32[2,8,128]{2,1,0:T(8,128)S(1)} %broadcast_maximum_fusion, f32[2,128,8]{1,2,0:T(8,128)S(1)} %bitcast.59), kind=kOutput, calls=%fused_computation.21 | convolution fusion | flops 34668544 | bytes 2637824 | tf_op jit(solution)/shard_map/shij,sjhd->shid/dot_general | solution.py:163
  174.2 1.1 copy.69
  175.3 2.0 %fusion.12 = bf16[2,128,256]{2,1,0:T(8,128)(2,1)} fusion(f32[2,128,256]{2,1,0:T(8,128)S(1)} %copy.69, bf16[2,128,256]{2,1,0:T(8,128)(2,1)S(1)} %copy-done.1, bf16[256,256]{1,0:T(8,128)(2,1)} %param.23, bf16[256,256]{1,0:T(8,128)(2,1)} %param.22, f32[2,128]{1,0:T(2,128)} %copy-done.5, f32[2,128]{1,0:T(2,128)} %copy-done.3), kind=kOutput, calls=%fused_computation.23 | convolution fusion | flops 67895296 | bytes 788480 | tf_op jit(solution)/shard_map/dot_general | solution.py:20
  177.3 1.6 copy.70
  (27 shorter events, 0.1 us)
Async XLA Ops:
  0.6 127.8 %copy-start = (bf16[1024,128]{1,0:T(8,128)(2,1)S(1)}, bf16[1024,128]{1,0:T(8,128)(2,1)}, u32[]{:S(2)}) copy-start(bf16[1024,128]{1,0:T(8,128)(2,1)} %param.18) | copy-start | bytes 786436
  3.3 163.3 %copy-start.3 = (f32[2,128]{1,0:T(2,128)}, f32[2,128]{1,0:T(2,128)S(1)}, u32[]{:S(2)}) copy-start(f32[2,128]{1,0:T(2,128)S(1)} %broadcast_multiply_fusion.1) | copy-start | bytes 3076
  4.4 162.2 %copy-start.5 = (f32[2,128]{1,0:T(2,128)}, f32[2,128]{1,0:T(2,128)S(1)}, u32[]{:S(2)}) copy-start(f32[2,128]{1,0:T(2,128)S(1)} %add_rsqrt_fusion.1) | copy-start | bytes 3076
  88.7 39.4 %copy-start.9 = (s32[4]{0:T(128)S(1)}, s32[4]{0:T(128)}, u32[]{:S(2)}) copy-start(s32[4]{0:T(128)} %param.14) | copy-start | bytes 52
  88.7 39.4 %copy-start.6 = (s32[16]{0:T(128)S(1)}, s32[16]{0:T(128)}, u32[]{:S(2)}) copy-start(s32[16]{0:T(128)} %param.15) | copy-start | bytes 196
  88.7 39.7 %copy-start.7 = (bf16[128,32,128]{2,1,0:T(8,128)(2,1)S(1)}, bf16[128,32,128]{2,1,0:T(8,128)(2,1)}, u32[]{:S(2)}) copy-start(bf16[128,32,128]{2,1,0:T(8,128)(2,1)} %param.13) | copy-start | bytes 3145732
  136.6 2.0 %copy-start.4 = (f32[128,8]{0,1:T(8,128)S(1)}, f32[128,8]{0,1:T(8,128)}, u32[]{:S(2)}) copy-start(f32[128,8]{0,1:T(8,128)} %param.19) | copy-start | bytes 12292
  138.5 17.7 %copy-start.1 = (bf16[2,128,256]{2,1,0:T(8,128)(2,1)S(1)}, bf16[2,128,256]{2,1,0:T(8,128)(2,1)}, u32[]{:S(2)}) copy-start(bf16[2,128,256]{2,1,0:T(8,128)(2,1)} %param.12) | copy-start | bytes 393220
  138.6 17.7 %copy-start.2 = (bf16[256,512]{1,0:T(8,128)(2,1)S(1)}, bf16[256,512]{1,0:T(8,128)(2,1)}, u32[]{:S(2)}) copy-start(bf16[256,512]{1,0:T(8,128)(2,1)} %param.21) | copy-start | bytes 786436
  154.8 11.8 %copy-start.8 = (bf16[256,256]{1,0:T(8,128)(2,1)S(1)}, bf16[256,256]{1,0:T(8,128)(2,1)}, u32[]{:S(2)}) copy-start(bf16[256,256]{1,0:T(8,128)(2,1)} %param.20) | copy-start | bytes 393220
where the time goes:
time: 182 us; the launch traced here: 179 us
  local copies, waits for them, and re-layouts  88.9 us (49%)
  blocking collectives  59.4 us (33%)
  matrix products  22.6 us (12%)
  other arithmetic  7.17 us (4%)
    transpose x1, local copies, waits for them, and re-layouts, outer_update(): outer.reshape(rows_here, width, cols_here, width).transpose(0, 2, 1, 3)  39.3 us
    reshape x1, local copies, waits for them, and re-layouts, outer_update(): outer.reshape(rows_here, width, cols_here, width).transpose(0, 2, 1, 3)  39.1 us
    all_gather x1, blocking collectives, per_device(): lax.all_gather(local_right_rows, 'row', axis=0, tiled=True)  15.6 us
    all_gather x1, blocking collectives, per_device(): bias_full = lax.all_gather(bias_local, 'row', axis=2, tiled=True)  14.9 us
    all_gather x1, blocking collectives, per_device(): lax.all_gather(local_left_rows, 'row', axis=0, tiled=True)  14.9 us
    all_gather x1, blocking collectives, per_device(): keyval_piece = lax.all_gather(local_key_value, 'col', axis=1, tiled=True)  8.43 us
    dot_general x1, matrix products, outer_update(): jnp.dot(outer, tensor_product_final, preferred_element_type=jnp.float32)  6.87 us
    dot_general x1, matrix products, outer_update(): jnp.dot(left_matrix, right_matrix, preferred_element_type=jnp.float32)  5.57 us

commit v1 on v0

v1 whole, which is shorter than its diff:
```python
import functools
import math

import jax
import jax.numpy as jnp
from jax import lax
from jax.experimental import pallas as pl
from jax.experimental.pallas import tpu as pltpu
from jax.sharding import PartitionSpec as P

EPS = 1e-05
MESH = pl.DeviceIdType.MESH
F32 = jnp.float32
BF16 = jnp.bfloat16


def standardize(values):
    center = values - jnp.mean(values, axis=-1, keepdims=True)
    spread = jnp.mean(center * center, axis=-1, keepdims=True)
    return center * lax.rsqrt(spread + EPS)


def dot_nt(a, b):
    return lax.dot_general(a, b, (((1,), (1,)), ((), ())), preferred_element_type=F32)


def dot_nn(a, b):
    return jnp.dot(a, b, preferred_element_type=F32)


def transposed(a):
    return a.astype(F32).T.astype(BF16)


def chain_of(position, start_ref, chains):
    chain = (position >= start_ref[0]).astype(jnp.int32)
    for k in range(1, chains):
        chain = chain + (position >= start_ref[k]).astype(jnp.int32)
    return chain - 1


def kernel(
    R, C,
    start_ref, label_ref, x_ref, couple_ref, wsrc_ref, wtgt_ref, wfin_ref, woff_ref,
    wq_ref, wkv_ref, wg_ref, wm_ref,
    out_ref, pair_ref,
    lsend, lall, rsend, rall, xall, lscr, rscr, wd, bscr, cf, biasf, ball,
    qbd, gt, kscr, vt, madd, gated,
    l_send, l_recv, r_send, r_recv, x_send, x_recv, b_send, b_recv, f_send, f_recv,
):
    SL, I, CH = x_ref.shape
    J, Z = couple_ref.shape[1], couple_ref.shape[2]
    S = label_ref.shape[0]
    chains = start_ref.shape[0]
    H = woff_ref.shape[1]
    PW = wsrc_ref.shape[1]
    inner = wq_ref.shape[1]
    D = inner // H
    A = C * I
    Q = I // J
    group = 128 // D
    halves = J // 16
    g = lax.axis_index("groups")
    r = lax.axis_index("row")
    c = lax.axis_index("col")
    n = R * C
    me = r * C + c

    barrier = pltpu.get_barrier_semaphore()

    def greet(k, carry):
        t = lax.rem(me + k, n)
        pl.semaphore_signal(
            barrier, inc=1, device_id=(g, lax.div(t, C), lax.rem(t, C)), device_id_type=MESH
        )
        return carry

    lax.fori_loop(1, n, greet, 0)

    xn = standardize(x_ref[...].astype(F32).reshape(SL * I, CH))
    chain_i = chain_of(
        c * I + lax.broadcasted_iota(jnp.int32, (I, CH), 0), start_ref, chains
    )
    labels = [label_ref[r * SL + s] for s in range(SL)]
    xm = []
    for s in range(SL):
        kept = jnp.logical_or(chain_i == labels[s], labels[s] == chains)
        xm.append(jnp.where(kept, xn[s * I : (s + 1) * I], 0.0).astype(BF16))
    xn = xn.astype(BF16)
    wsrc_t = transposed(wsrc_ref[...])
    for s in range(SL):
        lsend[s] = dot_nt(wsrc_t, xm[s]).astype(BF16)
    wt = wtgt_ref[...].astype(F32)
    wt = jnp.concatenate([wt] * (128 // PW), axis=1)
    wt_lane = lax.broadcasted_iota(jnp.int32, wt.shape, 1) // PW
    packed = None
    for half in range(halves):
        for s in range(SL):
            k = half * SL + s
            rows = xm[s].reshape(Q, halves, 16, CH)[:, half].reshape(Q * 16, CH)
            part = dot_nn(rows, jnp.where(wt_lane == k, wt, 0.0).astype(BF16))
            packed = part if packed is None else packed + part
    rsend[...] = packed.astype(BF16).reshape(Q, 16, 128)

    pl.semaphore_wait(barrier, n - 1)

    def copy_l(k):
        t = lax.rem(r + k, R)
        return pltpu.make_async_remote_copy(
            src_ref=lsend, dst_ref=lall.at[r], send_sem=l_send.at[k], recv_sem=l_recv.at[k],
            device_id=(g, t, c), device_id_type=MESH,
        )

    def copy_r(q, cc):
        return pltpu.make_async_remote_copy(
            src_ref=rsend.at[q], dst_ref=rall.at[r], send_sem=r_send.at[q * C + cc],
            recv_sem=r_recv.at[r], device_id=(g, c * Q + q, cc), device_id_type=MESH,
        )

    def copy_x(k):
        return pltpu.make_async_remote_copy(
            src_ref=x_ref, dst_ref=xall.at[c], send_sem=x_send.at[k], recv_sem=x_recv.at[k],
            device_id=(g, r, lax.rem(c + k, C)), device_id_type=MESH,
        )

    for q in range(Q):
        for cc in range(C):
            @pl.when(jnp.logical_not(jnp.logical_and(c * Q + q == r, cc == c)))
            def _(q=q, cc=cc):
                copy_r(q, cc).start()
    for k in range(1, R):
        copy_l(k).start()
    for k in range(1, C):
        copy_x(k).start()

    lall[r] = lsend[...]
    xall[c] = x_ref[...]
    own = lax.div(r, Q) == c

    @pl.when(own)
    def _():
        rall[r] = rsend[lax.rem(r, Q)]

    qt = dot_nt(transposed(wq_ref[...]), xn).astype(BF16)
    gate = jax.nn.sigmoid(dot_nt(transposed(wg_ref[...]), xn))
    row_block = lax.broadcasted_iota(jnp.int32, (128, I), 0) // D
    for s in range(SL):
        gt[s] = gate[:, s * I : (s + 1) * I]
        for h in range(H):
            base = (h // group) * 128
            piece = qt[base : base + 128, s * I : (s + 1) * I].astype(F32)
            qbd[s * H + h] = jnp.where(row_block == h % group, piece, 0.0).astype(BF16)
    for k in range(PW):
        piece = wfin_ref[k * PW : (k + 1) * PW, :]
        for m in range(128 // PW):
            wd[k // 2, m * PW : (m + 1) * PW, (k % 2) * Z : (k % 2 + 1) * Z] = piece
    cf[...] = couple_ref[...].astype(F32).reshape(I * J, Z)
    woff = woff_ref[...].T
    w1 = woff.astype(BF16).astype(F32)
    w2 = (woff - w1).astype(BF16).astype(F32)
    w3 = (woff - w1 - w2).astype(BF16).astype(F32)
    woff_t = jnp.concatenate([w1, w2, w3, jnp.zeros_like(w1)], axis=0).astype(BF16)

    members = []
    for k in range(chains + 1):
        total = (label_ref[0] == k).astype(jnp.int32)
        for s in range(1, S):
            total = total + (label_ref[s] == k).astype(jnp.int32)
        members.append(total)

    for k in range(R):
        @pl.when(jnp.logical_not(jnp.logical_and(own, r == k)))
        def _(k=k):
            pltpu.make_async_remote_copy(
                src_ref=rsend.at[0], dst_ref=rall.at[k], send_sem=r_send.at[0],
                recv_sem=r_recv.at[k], device_id=(g, r, c), device_id_type=MESH,
            ).wait_recv()
    lane = lax.broadcasted_iota(jnp.int32, (16, 128), 1) // PW
    for k in range(R):
        tile = rall[k].astype(F32)
        for half in range(halves):
            for s in range(SL):
                rscr[pl.ds(half * 16 * S + k * SL + s, 16, stride=S), :] = jnp.where(
                    lane == half * SL + s, tile, 0.0
                )
    right = rscr[...].astype(BF16)

    def spread_right(cp, carry):
        res = dot_nn(right, wd[cp]).astype(BF16)
        for j in range(J):
            for e in range(2):
                bscr[
                    j // 2,
                    pl.ds(pl.multiple_of((2 * cp + e) * S, 16), S),
                    (j % 2) * Z : (j % 2 + 1) * Z,
                ] = res[j * S : (j + 1) * S, e * Z : (e + 1) * Z]
        return carry

    lax.fori_loop(0, PW // 2, spread_right, 0)

    for k in range(1, R):
        copy_l(k).wait_recv()
    for k in range(R):
        for s in range(SL):
            piece = lall[k, s].astype(F32)
            for b in range(I // 128):
                at = pl.ds(b * PW * S + k * SL + s, PW, stride=S)
                lscr[at, :] = piece[:, b * 128 : (b + 1) * 128]
    left = jnp.concatenate(
        [lscr[b * PW * S : (b + 1) * PW * S, :].T for b in range(I // 128)], axis=0
    ).astype(BF16)

    chain_z = chain_i[:, :Z]

    def pair_step(jj, carry):
        update = dot_nn(left, bscr[jj])
        normed = []
        for e in range(2):
            j = 2 * jj + e
            chain_j = chain_of(r * J + j, start_ref, chains)
            own_rows = members[0]
            for k in range(1, chains):
                own_rows = jnp.where(chain_j == k, members[k], own_rows)
            same = 1.0 / (jnp.full((1, Z), members[chains] + own_rows, jnp.int32).astype(F32) + 0.001)
            other = 1.0 / (jnp.full((1, Z), members[chains], jnp.int32).astype(F32) + 0.001)
            factor = jnp.where(chain_z == chain_j, same, other)
            at = pl.ds(j, I, stride=J)
            state = (cf[at, :] + update[:, e * Z : (e + 1) * Z] * factor).astype(BF16).astype(F32)
            cf[at, :] = state
            normed.append(standardize(state).astype(BF16))
        res = dot_nt(woff_t, jnp.concatenate(normed, axis=0))
        res = res[:H] + res[H : 2 * H] + res[2 * H : 3 * H]
        for e in range(2):
            for b in range(I // 128):
                at = pl.ds(b * H * J + 2 * jj + e, H, stride=J)
                biasf[at, :] = res[:, e * I + b * 128 : e * I + (b + 1) * 128]
        return carry

    lax.fori_loop(0, J // 2, pair_step, 0)

    for b in range(I // 128):
        ball[r, :, :, b * 128 : (b + 1) * 128] = (
            biasf[b * H * J : (b + 1) * H * J, :].astype(BF16).reshape(H, J, 128)
        )

    ZC = R // 2
    z, core = lax.div(r, 2), lax.rem(r, 2)
    sibling = 2 * z + 1 - core

    def copy_b(k):
        return pltpu.make_async_remote_copy(
            src_ref=ball.at[r], dst_ref=ball.at[r], send_sem=b_send.at[k], recv_sem=b_recv.at[k],
            device_id=(g, 2 * lax.rem(z + k, ZC) + core, c), device_id_type=MESH,
        )

    def copy_f(k):
        slot = 2 * lax.rem(z + ZC - k, ZC) + core
        return pltpu.make_async_remote_copy(
            src_ref=ball.at[slot], dst_ref=ball.at[slot], send_sem=f_send.at[k],
            recv_sem=f_recv.at[k], device_id=(g, sibling, c), device_id_type=MESH,
        )

    for k in range(1, ZC):
        copy_b(k).start()
    copy_f(0).start()

    pair_ref[...] = cf[...].astype(BF16).reshape(I, J, Z)

    for k in range(1, C):
        copy_x(k).wait_recv()
    wv_t = transposed(wkv_ref[:, inner:])
    for cc in range(C):
        block = standardize(xall[cc].astype(F32).reshape(SL * I, CH)).astype(BF16)
        keys = dot_nn(block, wkv_ref[:, :inner]).astype(BF16)
        vals = dot_nt(wv_t, block).astype(BF16)
        for s in range(SL):
            kscr[s, cc * I : (cc + 1) * I, :] = keys[s * I : (s + 1) * I]
            vt[s, :, cc * I : (cc + 1) * I] = vals[:, s * I : (s + 1) * I]
    chain_a = chain_of(lax.broadcasted_iota(jnp.int32, (A, I), 0), start_ref, chains)
    for s in range(SL):
        kept = jnp.logical_or(chain_a == labels[s], labels[s] == chains)
        madd[s] = jnp.where(kept, 0.0, -1000000000.0)

    for k in range(1, ZC):
        copy_b(k).wait_recv()
        copy_f(k).start()
    for k in range(ZC):
        copy_f(k).wait_recv()

    scale = 1.0 / math.sqrt(D)

    def attend(step, carry):
        s, h = lax.div(step, H), lax.rem(step, H)
        at = pl.ds(pl.multiple_of(lax.div(h, group) * 128, 128), 128)
        scores = dot_nn(kscr[s, :, at], qbd[step]) * scale
        scores = scores + ball[:, h].astype(F32).reshape(A, I) + madd[s]
        weights = jnp.exp(scores - jnp.max(scores, axis=0, keepdims=True))
        total = jnp.sum(weights, axis=0, keepdims=True)
        rows = pl.ds(pl.multiple_of(h * D, D), D)
        attended = dot_nn(vt[s, rows, :], weights.astype(BF16)) / total
        gated[s, rows, :] = (gt[s, rows, :] * attended).astype(BF16)
        return carry

    lax.fori_loop(0, SL * H, attend, 0)

    for s in range(SL):
        merged = dot_nn(transposed(gated[s]), wm_ref[...])
        out_ref[s] = (x_ref[s].astype(F32) + merged).astype(BF16)

    for q in range(Q):
        for cc in range(C):
            @pl.when(jnp.logical_not(jnp.logical_and(c * Q + q == r, cc == c)))
            def _(q=q, cc=cc):
                copy_r(q, cc).wait_send()
    for k in range(1, R):
        copy_l(k).wait_send()
    for k in range(1, C):
        copy_x(k).wait_send()
    for k in range(1, ZC):
        copy_b(k).wait_send()
    for k in range(ZC):
        copy_f(k).wait_send()


def per_device(R, C, homolog, couple, starts, labels, *weights):
    SL, I, CH = homolog.shape
    J, Z = couple.shape[1], couple.shape[2]
    S = labels.shape[0]
    wsrc, wtgt, wfin, woff, wq = weights[:5]
    PW, H, inner = wsrc.shape[1], woff.shape[1], wq.shape[1]
    A = C * I
    Q = I // J
    vmem = pl.BlockSpec(memory_space=pltpu.VMEM)
    smem = pl.BlockSpec(memory_space=pltpu.SMEM)
    dma = pltpu.SemaphoreType.DMA
    return pl.pallas_call(
        functools.partial(kernel, R, C),
        out_shape=(
            jax.ShapeDtypeStruct(homolog.shape, BF16),
            jax.ShapeDtypeStruct(couple.shape, BF16),
        ),
        in_specs=[smem, smem] + [vmem] * 10,
        out_specs=(vmem, vmem),
        scratch_shapes=[
            pltpu.VMEM((SL, PW, I), BF16),
            pltpu.VMEM((R, SL, PW, I), BF16),
            pltpu.VMEM((Q, 16, 128), BF16),
            pltpu.VMEM((R, 16, 128), BF16),
            pltpu.VMEM((C, SL, I, CH), BF16),
            pltpu.VMEM((I // 128 * PW * S, 128), F32),
            pltpu.VMEM((J * S, 128), F32),
            pltpu.VMEM((PW // 2, 128, 2 * Z), BF16),
            pltpu.VMEM((J // 2, PW * S, 2 * Z), BF16),
            pltpu.VMEM((I * J, Z), F32),
            pltpu.VMEM((I // 128 * H * J, 128), F32),
            pltpu.VMEM((R, H, J, I), BF16),
            pltpu.VMEM((SL * H, 128, I), BF16),
            pltpu.VMEM((SL, inner, I), F32),
            pltpu.VMEM((SL, A, inner), BF16),
            pltpu.VMEM((SL, inner, A), BF16),
            pltpu.VMEM((SL, A, I), F32),
            pltpu.VMEM((SL, inner, I), BF16),
            dma((R,)), dma((R,)), dma((R,)), dma((R,)), dma((C,)), dma((C,)),
            dma((R // 2,)), dma((R // 2,)), dma((R // 2,)), dma((R // 2,)),
        ],
        compiler_params=pltpu.CompilerParams(
            collective_id=0, has_side_effects=True, vmem_limit_bytes=56 * 2**20
        ),
    )(starts, labels, homolog, couple, *weights)


def solution(mesh):
    spec = (
        P(("groups", "row"), "col", None),
        P(("groups", "col"), "row", None),
    )
    return jax.shard_map(
        functools.partial(per_device, mesh.shape["row"], mesh.shape["col"]),
        mesh=mesh,
        in_specs=spec + (P("groups"), P("groups")) + (P(),) * 8,
        out_specs=spec,
        check_vma=False,
    )
```

time: 182 us -> 46.5 us (0.26); the launches traced: 179 us -> 46.3 us
  local copies, waits for them, and re-layouts: 88.9 us -> 6.76 us
  blocking collectives: 59.4 us -> 0 us
  Pallas kernels: 0 us -> 38.8 us
  matrix products: 22.6 us -> 0 us
  other arithmetic: 7.17 us -> 0 us
    all_gather x5 -> x0, blocking collectives: 59.4 us -> none  [the longest x1 15.6 us: per_device(): lax.all_gather(local_right_rows, 'row', axis=0, tiled=True)]
    reshape x5 -> x0, local copies, waits for them, and re-layouts: 41.1 us -> none  [the longest x1 39.1 us: outer_update(): outer.reshape(rows_here, width, cols_here, width).transpose(0, 2, 1, 3)]
    transpose x3 -> x0, local copies, waits for them, and re-layouts: 39.8 us -> none  [the longest x1 39.3 us: outer_update(): outer.reshape(rows_here, width, cols_here, width).transpose(0, 2, 1, 3)]
    pallas_call x0 -> x1, Pallas kernels: none -> 38.8 us  [per_device(): pl.pallas_call(functools.partial(kernel, R, C), out_shape=(jax.ShapeDtype...]
    dot_general x11 -> x0, matrix products: 22.6 us -> none  [the longest x1 6.87 us: outer_update(): jnp.dot(outer, tensor_product_final, preferred_element_type=jnp.float32)]
    unnamed x21 -> x9, local copies, waits for them, and re-layouts: 1.7 us -> 6.76 us
    reduce_sum x7 -> x0, other arithmetic: 4.94 us -> none  [the longest x2 2.38 us: standardize_features(): spread = jnp.mean(center * center, axis=-1, keepdims=True)]
    slice x3 -> x0, local copies, waits for them, and re-layouts: 3.35 us -> none  [the longest x1 1.79 us: per_device(): keyval_piece[:, :, inner:]]
where the time goes in v1:
time: 46.5 us; the launch traced here: 46.3 us
  Pallas kernels  38.8 us (83%)
  local copies, waits for them, and re-layouts  6.76 us (15%)
  between operations  0.65 us (1%)
    pallas_call x1, Pallas kernels, per_device(): pl.pallas_call(functools.partial(kernel, R, C), out_shape=(jax.ShapeDtype...  38.8 us
    unnamed x9, local copies, waits for them, and re-layouts  6.76 us

profile of v1, /device:TPU:1, one launch (start us, length us, event | category | flops | bytes accessed | tf_op | source)
XLA Modules:
  0.0 46.3 jit_solution(1992881250888552435)
XLA Ops:
  0.6 0.0 copy-start
  0.6 1.5 %copy.14.wsrc_ref = bf16[256,32]{1,0:T(8,128)(2,1)} copy(bf16[256,32]{0,1:T(8,128)(2,1)} %param.16) | data formatting | bytes 32768 | tf_op args[4]
  2.1 0.0 copy-done
  2.1 0.0 copy-start.1
  2.1 0.7 %copy.15.wtgt_ref = bf16[256,32]{1,0:T(8,128)(2,1)} copy(bf16[256,32]{0,1:T(8,128)(2,1)S(1)} %copy-done) | data formatting | bytes 32768 | tf_op args[5]
  2.8 0.0 copy-done.1
  2.8 0.7 %copy.16.woff_ref = f32[128,8]{1,0:T(8,128)} copy(f32[128,8]{0,1:T(8,128)S(1)} %copy-done.1) | data formatting | bytes 8192 | tf_op args[7]
  3.6 38.8 %shard_map.131 = (bf16[2,128,256]{2,1,0:T(8,128)(2,1)}, bf16[128,32,128]{2,1,0:T(8,128)(2,1)}) custom-call(s32[4]{0:T(128)} %start_ref.1, s32[16]{0:T(128)} %label_ref.1, bf16[2,128,256]{2,1,0:T(8,128)(2,1)} %x_ref.1, bf16[128,32,128]{2,1,0:T(8,128)(2,1)} %couple_ref.1, bf16[256,32]{1,0:T(8,128)(2,1)} %copy.14.wsrc_ref, bf16[256,32]{1,0:T(8,128)(2,1)} %copy.15.wtgt_ref, ...), custom_call_target="tpu_custom_call" | custom-call | tf_op jit(solution)/shard_map/pallas_call | solution.py:336
  42.4 1.6 %copy.19 = bf16[2,128,256]{2,1,0:T(8,128)(2,1)} copy(bf16[2,128,256]{2,1,0:T(8,128)(2,1)} %get-tuple-element.4) | data formatting | bytes 262144
  44.0 2.3 %copy.20 = bf16[128,32,128]{2,1,0:T(8,128)(2,1)} copy(bf16[128,32,128]{2,1,0:T(8,128)(2,1)} %get-tuple-element.5) | data formatting | bytes 2097152
Async XLA Ops:
  0.6 1.5 %copy-start = (bf16[256,32]{0,1:T(8,128)(2,1)S(1)}, bf16[256,32]{0,1:T(8,128)(2,1)}, u32[]{:S(2)}) copy-start(bf16[256,32]{0,1:T(8,128)(2,1)} %param.17) | copy-start | bytes 49156
  2.1 0.7 %copy-start.1 = (f32[128,8]{0,1:T(8,128)S(1)}, f32[128,8]{0,1:T(8,128)}, u32[]{:S(2)}) copy-start(f32[128,8]{0,1:T(8,128)} %param.19) | copy-start | bytes 12292

commit v2 on v1

--- a/solution.py
+++ b/solution.py
@@ -12,6 +12,7 @@
 MESH = pl.DeviceIdType.MESH
 F32 = jnp.float32
 BF16 = jnp.bfloat16
+UP, US, UA, UB = 4, 4, 4, 4
 
 
 def standardize(values):
@@ -45,15 +46,15 @@
     wq_ref, wkv_ref, wg_ref, wm_ref,
     out_ref, pair_ref,
     lsend, lall, rsend, rall, xall, lscr, rscr, wd, bscr, cf, biasf, ball,
-    qbd, gt, kscr, vt, madd, gated,
+    qbd, gt, kscr, vt, madd, gated, held,
     l_send, l_recv, r_send, r_recv, x_send, x_recv, b_send, b_recv, f_send, f_recv,
 ):
     SL, I, CH = x_ref.shape
     J, Z = couple_ref.shape[1], couple_ref.shape[2]
     S = label_ref.shape[0]
     chains = start_ref.shape[0]
-    H = woff_ref.shape[1]
-    PW = wsrc_ref.shape[1]
+    H = woff_ref.shape[0]
+    PW = wsrc_ref.shape[0]
     inner = wq_ref.shape[1]
     D = inner // H
     A = C * I
@@ -87,18 +88,18 @@
         kept = jnp.logical_or(chain_i == labels[s], labels[s] == chains)
         xm.append(jnp.where(kept, xn[s * I : (s + 1) * I], 0.0).astype(BF16))
     xn = xn.astype(BF16)
-    wsrc_t = transposed(wsrc_ref[...])
+    wsrc_t = wsrc_ref[...]
     for s in range(SL):
         lsend[s] = dot_nt(wsrc_t, xm[s]).astype(BF16)
     wt = wtgt_ref[...].astype(F32)
-    wt = jnp.concatenate([wt] * (128 // PW), axis=1)
-    wt_lane = lax.broadcasted_iota(jnp.int32, wt.shape, 1) // PW
+    wt = jnp.concatenate([wt] * (128 // PW), axis=0)
+    wt_row = lax.broadcasted_iota(jnp.int32, wt.shape, 0) // PW
     packed = None
     for half in range(halves):
         for s in range(SL):
             k = half * SL + s
             rows = xm[s].reshape(Q, halves, 16, CH)[:, half].reshape(Q * 16, CH)
-            part = dot_nn(rows, jnp.where(wt_lane == k, wt, 0.0).astype(BF16))
+            part = dot_nt(rows, jnp.where(wt_row == k, wt, 0.0).astype(BF16))
             packed = part if packed is None else packed + part
     rsend[...] = packed.astype(BF16).reshape(Q, 16, 128)
 
@@ -155,7 +156,7 @@
         for m in range(128 // PW):
             wd[k // 2, m * PW : (m + 1) * PW, (k % 2) * Z : (k % 2 + 1) * Z] = piece
     cf[...] = couple_ref[...].astype(F32).reshape(I * J, Z)
-    woff = woff_ref[...].T
+    woff = woff_ref[...]
     w1 = woff.astype(BF16).astype(F32)
     w2 = (woff - w1).astype(BF16).astype(F32)
     w3 = (woff - w1 - w2).astype(BF16).astype(F32)
@@ -196,7 +197,7 @@
                 ] = res[j * S : (j + 1) * S, e * Z : (e + 1) * Z]
         return carry
 
-    lax.fori_loop(0, PW // 2, spread_right, 0)
+    lax.fori_loop(0, PW // 2, spread_right, 0, unroll=UB)
 
     for k in range(1, R):
         copy_l(k).wait_recv()
@@ -232,37 +233,38 @@
         res = res[:H] + res[H : 2 * H] + res[2 * H : 3 * H]
         for e in range(2):
             for b in range(I // 128):
-                at = pl.ds(b * H * J + 2 * jj + e, H, stride=J)
+                at = pl.ds(b * H * 16 + lax.rem(2 * jj, 16) + e, H, stride=16)
                 biasf[at, :] = res[:, e * I + b * 128 : e * I + (b + 1) * 128]
         return carry
-
-    lax.fori_loop(0, J // 2, pair_step, 0)
-
-    for b in range(I // 128):
-        ball[r, :, :, b * 128 : (b + 1) * 128] = (
-            biasf[b * H * J : (b + 1) * H * J, :].astype(BF16).reshape(H, J, 128)
-        )
 
     ZC = R // 2
     z, core = lax.div(r, 2), lax.rem(r, 2)
     sibling = 2 * z + 1 - core
 
-    def copy_b(k):
-        return pltpu.make_async_remote_copy(
-            src_ref=ball.at[r], dst_ref=ball.at[r], send_sem=b_send.at[k], recv_sem=b_recv.at[k],
+    def copy_b(half, k):
+        return pltpu.make_async_remote_copy(
+            src_ref=ball.at[r, half], dst_ref=ball.at[r, half],
+            send_sem=b_send.at[half, k], recv_sem=b_recv.at[half, k],
             device_id=(g, 2 * lax.rem(z + k, ZC) + core, c), device_id_type=MESH,
         )
 
-    def copy_f(k):
+    def copy_f(half, k):
         slot = 2 * lax.rem(z + ZC - k, ZC) + core
         return pltpu.make_async_remote_copy(
-            src_ref=ball.at[slot], dst_ref=ball.at[slot], send_sem=f_send.at[k],
-            recv_sem=f_recv.at[k], device_id=(g, sibling, c), device_id_type=MESH,
-        )
-
-    for k in range(1, ZC):
-        copy_b(k).start()
-    copy_f(0).start()
+            src_ref=ball.at[slot, half], dst_ref=ball.at[slot, half],
+            send_sem=f_send.at[half, k], recv_sem=f_recv.at[half, k],
+            device_id=(g, sibling, c), device_id_type=MESH,
+        )
+
+    for half in range(halves):
+        lax.fori_loop(half * 8, half * 8 + 8, pair_step, 0, unroll=UP)
+        for b in range(I // 128):
+            ball[r, half, :, :, b * 128 : (b + 1) * 128] = (
+                biasf[b * H * 16 : (b + 1) * H * 16, :].astype(BF16).reshape(H, 16, 128)
+            )
+        for k in range(1, ZC):
+            copy_b(half, k).start()
+        copy_f(half, 0).start()
 
     pair_ref[...] = cf[...].astype(BF16).reshape(I, J, Z)
 
@@ -281,19 +283,30 @@
         kept = jnp.logical_or(chain_a == labels[s], labels[s] == chains)
         madd[s] = jnp.where(kept, 0.0, -1000000000.0)
 
-    for k in range(1, ZC):
-        copy_b(k).wait_recv()
-        copy_f(k).start()
-    for k in range(ZC):
-        copy_f(k).wait_recv()
-
     scale = 1.0 / math.sqrt(D)
+
+    def score(step, carry):
+        s, h = lax.div(step, H), lax.rem(step, H)
+        at = pl.ds(pl.multiple_of(lax.div(h, group) * 128, 128), 128)
+        held[step] = dot_nn(kscr[s, :, at], qbd[step]) * scale + madd[s]
+        return carry
+
+    def forward(half):
+        for k in range(1, ZC):
+            copy_b(half, k).wait_recv()
+            copy_f(half, k).start()
+
+    for half in range(halves - 1):
+        forward(half)
+    lax.fori_loop(0, SL * H, score, 0, unroll=US)
+    forward(halves - 1)
+    for half in range(halves):
+        for k in range(ZC):
+            copy_f(half, k).wait_recv()
 
     def attend(step, carry):
         s, h = lax.div(step, H), lax.rem(step, H)
-        at = pl.ds(pl.multiple_of(lax.div(h, group) * 128, 128), 128)
-        scores = dot_nn(kscr[s, :, at], qbd[step]) * scale
-        scores = scores + ball[:, h].astype(F32).reshape(A, I) + madd[s]
+        scores = held[step] + ball[:, :, h].astype(F32).reshape(A, I)
         weights = jnp.exp(scores - jnp.max(scores, axis=0, keepdims=True))
         total = jnp.sum(weights, axis=0, keepdims=True)
         rows = pl.ds(pl.multiple_of(h * D, D), D)
@@ -301,7 +314,7 @@
         gated[s, rows, :] = (gt[s, rows, :] * attended).astype(BF16)
         return carry
 
-    lax.fori_loop(0, SL * H, attend, 0)
+    lax.fori_loop(0, SL * H, attend, 0, unroll=UA)
 
     for s in range(SL):
         merged = dot_nn(transposed(gated[s]), wm_ref[...])
@@ -316,10 +329,11 @@
         copy_l(k).wait_send()
     for k in range(1, C):
         copy_x(k).wait_send()
-    for k in range(1, ZC):
-        copy_b(k).wait_send()
-    for k in range(ZC):
-        copy_f(k).wait_send()
+    for half in range(halves):
+        for k in range(1, ZC):
+            copy_b(half, k).wait_send()
+        for k in range(ZC):
+            copy_f(half, k).wait_send()
 
 
 def per_device(R, C, homolog, couple, starts, labels, *weights):
@@ -352,21 +366,22 @@
             pltpu.VMEM((PW // 2, 128, 2 * Z), BF16),
             pltpu.VMEM((J // 2, PW * S, 2 * Z), BF16),
             pltpu.VMEM((I * J, Z), F32),
-            pltpu.VMEM((I // 128 * H * J, 128), F32),
-            pltpu.VMEM((R, H, J, I), BF16),
+            pltpu.VMEM((I // 128 * H * 16, 128), F32),
+            pltpu.VMEM((R, J // 16, H, 16, I), BF16),
             pltpu.VMEM((SL * H, 128, I), BF16),
             pltpu.VMEM((SL, inner, I), F32),
             pltpu.VMEM((SL, A, inner), BF16),
             pltpu.VMEM((SL, inner, A), BF16),
             pltpu.VMEM((SL, A, I), F32),
             pltpu.VMEM((SL, inner, I), BF16),
+            pltpu.VMEM((SL * H, A, I), F32),
             dma((R,)), dma((R,)), dma((R,)), dma((R,)), dma((C,)), dma((C,)),
-            dma((R // 2,)), dma((R // 2,)), dma((R // 2,)), dma((R // 2,)),
+            *[dma((J // 16, R // 2))] * 4,
         ],
         compiler_params=pltpu.CompilerParams(
-            collective_id=0, has_side_effects=True, vmem_limit_bytes=56 * 2**20
+            collective_id=0, has_side_effects=True, vmem_limit_bytes=61 * 2**20
         ),
-    )(starts, labels, homolog, couple, *weights)
+    )(starts, labels, homolog, couple, wsrc.T, wtgt.T, wfin, woff.T, *weights[4:])
 
 
 def solution(mesh):

time: 46.5 us -> 34.5 us (0.74)
  Pallas kernels: 38.8 us -> 29.9 us
  local copies, waits for them, and re-layouts: 6.76 us -> 3.83 us
    pallas_call x1, Pallas kernels: 38.8 us -> 29.9 us  [per_device(): pl.pallas_call(functools.partial(kernel, R, C), out_shape=(jax.ShapeDtype...]
    unnamed x9 -> x2, local copies, waits for them, and re-layouts: 6.76 us -> 3.83 us
where the time goes in v2:
time: 34.5 us; the launch traced here: 34.3 us
  Pallas kernels  29.9 us (87%)
  local copies, waits for them, and re-layouts  3.83 us (11%)
  between operations  0.64 us (2%)
    pallas_call x1, Pallas kernels, per_device(): pl.pallas_call(functools.partial(kernel, R, C), out_shape=(jax.ShapeDtype...  29.9 us
    unnamed x2, local copies, waits for them, and re-layouts  3.83 us

profile of v2, /device:TPU:1, one launch (start us, length us, event | category | flops | bytes accessed | tf_op | source)
XLA Modules:
  0.0 34.3 jit_solution(11765860740150539112)
XLA Ops:
  0.6 29.9 %shard_map.131 = (bf16[2,128,256]{2,1,0:T(8,128)(2,1)}, bf16[128,32,128]{2,1,0:T(8,128)(2,1)}) custom-call(s32[4]{0:T(128)} %start_ref.1, s32[16]{0:T(128)} %label_ref.1, bf16[2,128,256]{2,1,0:T(8,128)(2,1)} %x_ref.1, bf16[128,32,128]{2,1,0:T(8,128)(2,1)} %couple_ref.1, bf16[32,256]{1,0:T(8,128)(2,1)} %bitcast.3, bf16[32,256]{1,0:T(8,128)(2,1)} %bitcast.4, ...), custom_call_target="tpu_custom_call" | custom-call | tf_op jit(solution)/shard_map/pallas_call | solution.py:350
  30.5 1.6 %copy.16 = bf16[2,128,256]{2,1,0:T(8,128)(2,1)} copy(bf16[2,128,256]{2,1,0:T(8,128)(2,1)} %get-tuple-element.4) | data formatting | bytes 262144
  32.1 2.3 %copy.17 = bf16[128,32,128]{2,1,0:T(8,128)(2,1)} copy(bf16[128,32,128]{2,1,0:T(8,128)(2,1)} %get-tuple-element.5) | data formatting | bytes 2097152

commit v3 on v2

--- a/solution.py
+++ b/solution.py
@@ -12,7 +12,7 @@
 MESH = pl.DeviceIdType.MESH
 F32 = jnp.float32
 BF16 = jnp.bfloat16
-UP, US, UA, UB = 4, 4, 4, 4
+UP, US, UA, UB = 8, 4, 8, 8
 
 
 def standardize(values):

time: 34.5 us -> 33.6 us (0.974)
  Pallas kernels: 29.9 us -> 28.9 us
    pallas_call x1, Pallas kernels: 29.9 us -> 28.9 us  [per_device(): pl.pallas_call(functools.partial(kernel, R, C), out_shape=(jax.ShapeDtype...]
where the time goes in v3:
time: 33.6 us; the launch traced here: 33.4 us
  Pallas kernels  28.9 us (86%)
  local copies, waits for them, and re-layouts  3.83 us (11%)
  between operations  0.64 us (2%)
    pallas_call x1, Pallas kernels, per_device(): pl.pallas_call(functools.partial(kernel, R, C), out_shape=(jax.ShapeDtype...  28.9 us
    unnamed x2, local copies, waits for them, and re-layouts  3.83 us

profile of v3, /device:TPU:1, one launch (start us, length us, event | category | flops | bytes accessed | tf_op | source)
XLA Modules:
  0.0 33.4 jit_solution(7864129734181884305)
XLA Ops:
  0.6 28.9 %shard_map.131 = (bf16[2,128,256]{2,1,0:T(8,128)(2,1)}, bf16[128,32,128]{2,1,0:T(8,128)(2,1)}) custom-call(s32[4]{0:T(128)} %start_ref.1, s32[16]{0:T(128)} %label_ref.1, bf16[2,128,256]{2,1,0:T(8,128)(2,1)} %x_ref.1, bf16[128,32,128]{2,1,0:T(8,128)(2,1)} %couple_ref.1, bf16[32,256]{1,0:T(8,128)(2,1)} %bitcast.3, bf16[32,256]{1,0:T(8,128)(2,1)} %bitcast.4, ...), custom_call_target="tpu_custom_call" | custom-call | tf_op jit(solution)/shard_map/pallas_call | solution.py:350
  29.6 1.6 %copy.16 = bf16[2,128,256]{2,1,0:T(8,128)(2,1)} copy(bf16[2,128,256]{2,1,0:T(8,128)(2,1)} %get-tuple-element.4) | data formatting | bytes 262144
  31.1 2.3 %copy.17 = bf16[128,32,128]{2,1,0:T(8,128)(2,1)} copy(bf16[128,32,128]{2,1,0:T(8,128)(2,1)} %get-tuple-element.5) | data formatting | bytes 2097152

commit v4 on v3

--- a/solution.py
+++ b/solution.py
@@ -266,6 +266,14 @@
             copy_b(half, k).start()
         copy_f(half, 0).start()
 
+    def forward(half):
+        for k in range(1, ZC):
+            copy_b(half, k).wait_recv()
+            copy_f(half, k).start()
+
+    for half in range(halves - 1):
+        forward(half)
+
     pair_ref[...] = cf[...].astype(BF16).reshape(I, J, Z)
 
     for k in range(1, C):
@@ -291,13 +299,6 @@
         held[step] = dot_nn(kscr[s, :, at], qbd[step]) * scale + madd[s]
         return carry
 
-    def forward(half):
-        for k in range(1, ZC):
-            copy_b(half, k).wait_recv()
-            copy_f(half, k).start()
-
-    for half in range(halves - 1):
-        forward(half)
     lax.fori_loop(0, SL * H, score, 0, unroll=US)
     forward(halves - 1)
     for half in range(halves):

time: 33.6 us -> 33.6 us (level)
  no operation moved by 1% of the time
where the time goes in v4:
time: 33.6 us; the launch traced here: 33.4 us
  Pallas kernels  28.9 us (86%)
  local copies, waits for them, and re-layouts  3.83 us (11%)
  between operations  0.64 us (2%)
    pallas_call x1, Pallas kernels, per_device(): pl.pallas_call(functools.partial(kernel, R, C), out_shape=(jax.ShapeDtype...  28.9 us
    unnamed x2, local copies, waits for them, and re-layouts  3.83 us

profile of v4, /device:TPU:1, one launch (start us, length us, event | category | flops | bytes accessed | tf_op | source)
XLA Modules:
  0.0 33.4 jit_solution(11734621473480015345)
XLA Ops:
  0.6 28.9 %shard_map.131 = (bf16[2,128,256]{2,1,0:T(8,128)(2,1)}, bf16[128,32,128]{2,1,0:T(8,128)(2,1)}) custom-call(s32[4]{0:T(128)} %start_ref.1, s32[16]{0:T(128)} %label_ref.1, bf16[2,128,256]{2,1,0:T(8,128)(2,1)} %x_ref.1, bf16[128,32,128]{2,1,0:T(8,128)(2,1)} %couple_ref.1, bf16[32,256]{1,0:T(8,128)(2,1)} %bitcast.3, bf16[32,256]{1,0:T(8,128)(2,1)} %bitcast.4, ...), custom_call_target="tpu_custom_call" | custom-call | tf_op jit(solution)/shard_map/pallas_call | solution.py:351
  29.6 1.6 %copy.16 = bf16[2,128,256]{2,1,0:T(8,128)(2,1)} copy(bf16[2,128,256]{2,1,0:T(8,128)(2,1)} %get-tuple-element.4) | data formatting | bytes 262144
  31.1 2.3 %copy.17 = bf16[128,32,128]{2,1,0:T(8,128)(2,1)} copy(bf16[128,32,128]{2,1,0:T(8,128)(2,1)} %get-tuple-element.5) | data formatting | bytes 2097152
